TPU v7x, 768 devices: a whole 4x8x12 slice. The times are simulated.
768 devices in a mesh: wide: 64 (over y, x, core), grp: 12 (over z).
Axes of the slice: x: 4, y: 8, z: 12, core: 2. Of those that a mesh axis runs over, the one named last changes fastest.
Arguments:
- table: bfloat16 [786432, 256], P(('wide', 'grp')), may hold values from -4 to 4
- item_weight: bfloat16 [256, 1024], replicated, may hold values from -1.5 to 1.5
- ids: int32 [393216], P(('wide', 'grp')), may hold values from 0 to 786431, as said below
- queries: bfloat16 [24576, 1024], P(('wide', 'grp')), may hold values from -7 to 7
- memory: bfloat16 [3, 24576, 1024], P(None, ('wide', 'grp')), may hold values from -4 to 4
- slot_age: int32 [3, 24576], P(None, ('wide', 'grp')), may hold values from 0 to 5
- positive: int32 [768, 32], P(('wide', 'grp')), may hold values from 0 to 31, each once within a row
Outputs:
- loss: float32 [24576], P(('wide', 'grp'))
- table_grad: float32 [786432, 256], P(('wide', 'grp'))
Inputs may be any that keep to these rules, and one draw needn't show every extreme that they name: The ids of a device name rows of exactly four devices with the device's wide index, exactly 128 ids for each of the four; one of the four is the same for all devices of one wide index. Ids may repeat. `slot_age`: only whether an age is at most 3 matters; ages may travel in any encoding.
All inputs are finite; a program needn't handle non-finite values.
Results may differ from a plain program's by a relative error of at most 0.0007.
The roundings to bfloat16 on the way count: a program that leaves them out, or rounds other values in their place, can miss the bound.
Values may be sent and summed in bfloat16 or wider, within the bound.
A program may use at most 64 MiB of HBM per device.

v0:
```python
import math

import jax
import jax.numpy as jnp
from jax import lax
from jax.sharding import PartitionSpec as P


def body(table, item_weight, ids, queries, memory, slot_age, positive):
    groups = lax.axis_size("grp")
    per_device = queries.shape[0]
    rows_dev = table.shape[0]
    ids_dev = ids.shape[0]
    bag_size = ids_dev // per_device
    capacity = ids_dev // 4
    emb_width = table.shape[1]
    steps_held = memory.shape[0]
    factor = 2.0 / math.sqrt(queries.shape[1])
    owner_grp = ids // rows_dev % groups
    local_row = ids % rows_dev
    onehot = (owner_grp[:, None] == jnp.arange(groups, dtype=jnp.int32)[None, :]).astype(jnp.int32)
    before = jnp.cumsum(onehot, axis=0) - onehot
    placed = owner_grp * capacity + jnp.sum(before * onehot, axis=1)
    requests = (
        jnp.full((groups * capacity,), -1, jnp.int32)
        .at[placed]
        .set(local_row)
        .reshape(groups, capacity)
    )
    asked = lax.all_to_all(requests, "grp", split_axis=0, concat_axis=0, tiled=True)
    found = table[jnp.maximum(asked, 0)]
    found = jnp.where((asked >= 0)[..., None], found, jnp.zeros_like(found))
    fetched = lax.all_to_all(found, "grp", split_axis=0, concat_axis=0, tiled=True)
    looked = fetched.reshape(groups * capacity, emb_width)[placed]
    pooled = (
        jnp.sum(looked.astype(jnp.float32).reshape(per_device, bag_size, emb_width), axis=1)
        / bag_size
    ).astype(jnp.bfloat16)
    items = jnp.dot(pooled, item_weight, preferred_element_type=jnp.float32).astype(jnp.bfloat16)
    own_scores = (
        jnp.einsum("qd,kd->qk", queries, items, preferred_element_type=jnp.float32) * factor
    )
    highest = jnp.full((per_device,), -jnp.inf, jnp.float32)
    summed = jnp.zeros((per_device,), jnp.float32)
    scores = (
        jnp.einsum(
            "qd,kd->qk",
            queries,
            lax.all_gather(items, "wide", axis=0, tiled=True),
            preferred_element_type=jnp.float32,
        )
        * factor
    )
    new_high = jnp.max(scores, axis=1)
    summed = summed * jnp.exp(highest - new_high) + jnp.sum(
        jnp.exp(scores - new_high[:, None]), axis=1
    )
    stale_rows = lax.all_gather(memory, "wide", axis=1, tiled=True)
    slot_ages = lax.all_gather(slot_age, "wide", axis=1, tiled=True)
    highest, summed = (new_high, summed)
    scores = (
        jnp.einsum("qd,snd->qsn", queries, stale_rows, preferred_element_type=jnp.float32) * factor
    )
    alive = (slot_ages <= steps_held)[None]
    new_high = jnp.maximum(highest, jnp.max(jnp.where(alive, scores, -jnp.inf), axis=(1, 2)))
    summed = summed * jnp.exp(highest - new_high)
    summed = summed + jnp.sum(
        jnp.where(alive, jnp.exp(scores - new_high[:, None, None]), 0.0), axis=(1, 2)
    )
    highest, summed = (new_high, summed)
    lse = highest + jnp.log(summed)
    labels = positive[0]
    chosen = labels[:, None] == jnp.arange(per_device, dtype=jnp.int32)[None, :]
    loss = lse - jnp.sum(jnp.where(chosen, own_scores, 0.0), axis=1)
    coef = (jnp.exp(own_scores - lse[:, None]) - chosen.astype(jnp.float32)).astype(jnp.bfloat16)
    item_grad = (
        jnp.einsum("qk,qd->kd", coef, queries, preferred_element_type=jnp.float32) * factor
    ).astype(jnp.bfloat16)
    pooled_grad = jnp.einsum(
        "kd,ed->ke", item_grad, item_weight, preferred_element_type=jnp.float32
    )
    id_grad = jnp.repeat(pooled_grad, bag_size, axis=0) / bag_size
    outgoing = (
        jnp.zeros((groups * capacity, emb_width), jnp.float32)
        .at[placed]
        .set(id_grad)
        .reshape(groups, capacity, emb_width)
    )
    incoming = lax.all_to_all(outgoing, "grp", split_axis=0, concat_axis=0, tiled=True)
    targets = jnp.maximum(asked, 0).reshape(-1)
    table_grad = (
        jnp.zeros((rows_dev, emb_width), jnp.float32)
        .at[targets]
        .add(incoming.reshape(-1, emb_width))
    )
    return (loss, table_grad)


def solution(mesh):
    placed = (
        P(("wide", "grp"), None),
        P(),
        P(("wide", "grp")),
        P(("wide", "grp"), None),
        P(None, ("wide", "grp"), None),
        P(None, ("wide", "grp")),
        P(("wide", "grp"), None),
    )
    return jax.shard_map(
        body,
        mesh=mesh,
        in_specs=placed,
        out_specs=(P(("wide", "grp")), P(("wide", "grp"), None)),
        check_vma=False,
    )
```

profile of v0, /device:TPU:1, one launch (start us, length us, event | category | flops | bytes accessed | tf_op | source)
XLA Modules:
  0.0 366.0 jit_solution(770325609958941711)
XLA Ops:
  7.2 0.8 add_select_fusion
  8.0 1.2 reduce-window.6
  9.1 0.2 slice_reduce_fusion
  9.4 0.1 broadcast_add_fusion
  9.5 2.5 scatter_custom_fusion
  12.0 24.4 %all_to_all.19 = s32[12,1,128]{2,1,0:T(1,128)S(1)} all-to-all(s32[12,1,128]{2,1,0:T(1,128)S(1)} %all_to_all.12), channel_id=1, replica_groups=mesh['wide'=64,'grp'=12] {'grp'}, dimensions={0} | all-to-all | bytes 12288 | tf_op jit(solution)/shard_map/all_to_all | solution.py:30
  36.5 4.8 %gather_fusion = bf16[1536,256]{1,0:T(8,128)(2,1)S(1)} fusion(bf16[1024,256]{1,0:T(8,128)(2,1)S(1)} %copy-done, s32[2048]{0:T(1024)S(1)} %pad_clamp_fusion), kind=kCustom, calls=%fused_computation | custom fusion | bytes 1579008 | tf_op jit(solution)/shard_map/gather | solution.py:31
  41.2 1.2 broadcast_select_fusion
  42.4 3.7 all-to-all-start.1
  46.1 0.0 all-gather.4.cloned.1.call-start
  46.1 27.7 %all-to-all-done.1 = bf16[12,128,256]{2,1,0:T(8,128)(2,1)S(1)} async-done(((bf16[12,128,256]{2,1,0:T(8,128)(2,1)}), bf16[12,128,256]{2,1,0:T(8,128)(2,1)S(1)}, u32[]{:S(2)}, u32[]{:S(2)}) %all-to-all-start.1) | async-done | bytes 786464 | tf_op jit(solution)/shard_map/all_to_all | solution.py:33
  73.9 1.9 gather_fusion.1
  75.8 0.1 convert_reduce_fusion
  75.9 0.8 convolution_convert_fusion
  76.8 0.0 all-gather.6.cloned.1.call-start
  76.8 0.7 all-gather.6.cloned.1.call-update
  77.5 57.5 %all-gather = s32[64,32,3]{1,2,0:T(4,128)S(1)} all-gather(s32[1,32,3]{1,2,0:T(4,128)S(1)} %bitcast.56), channel_id=1, replica_groups=mesh['wide'=64,'grp'=12] {'wide'}, dimensions={0}, use_global_device_ids=true | all-gather | bytes 24960 | tf_op jit(solution)/shard_map/all_gather | solution.py:59
  135.1 0.1 copy.20
  135.2 0.1 copy.21
  135.3 0.1 reshape.154
  135.4 1.0 select_reduce_fusion.2
  136.4 30.5 %all-gather.4.cloned.1.call-done = bf16[2048,1024]{1,0:T(8,128)(2,1)} async-done(((bf16[32,1024]{1,0:T(8,128)(2,1)}), bf16[2048,1024]{1,0:T(8,128)(2,1)}) %all-gather.4.cloned.1.call-update) | async-done | bytes 4194320 | tf_op jit(solution)/shard_map/all_gather | solution.py:49
  167.0 3.6 fusion.27
  170.6 0.2 exponential_reduce_fusion
  170.8 98.3 %all-gather.6.cloned.1.call-done = bf16[3,2048,1024]{2,1,0:T(8,128)(2,1)} async-done(((bf16[3,32,1024]{2,1,0:T(8,128)(2,1)}), bf16[3,2048,1024]{2,1,0:T(8,128)(2,1)}) %all-gather.6.cloned.1.call-update) | async-done | bytes 12582928 | tf_op jit(solution)/shard_map/all_gather | solution.py:58
  269.2 8.5 %select_reduce_fusion.1 = (f32[32]{0:T(128)S(1)}, f32[32,3,2048]{2,0,1:T(8,128)S(1)}) fusion(pred[3,2048]{1,0:T(4,128)(4,1)S(1)} %bitcast.53, bf16[3,2048,1024]{2,1,0:T(8,128)(2,1)} %all-gather.6.cloned.1.call-done, bf16[32,1024]{1,0:T(8,128)(2,1)S(1)} %copy-done.2), kind=kOutput, calls=%fused_computation.17 | convolution fusion | flops 403242976 | bytes 13441152 | tf_op jit(solution)/shard_map/qd,snd->qsn/dot_general | solution.py:62
  277.6 0.3 select_reduce_fusion
  278.0 0.5 fusion.26
  278.5 0.3 fusion.2
  278.9 2.6 scatter_custom_fusion.1
  281.6 66.0 %all_to_all.20 = f32[12,128,256]{2,1,0:T(8,128)} all-to-all(f32[12,128,256]{2,1,0:T(8,128)S(1)} %bitcast.47), channel_id=1, replica_groups=mesh['wide'=64,'grp'=12] {'grp'}, dimensions={0} | all-to-all | bytes 3145728 | tf_op jit(solution)/shard_map/all_to_all | solution.py:89
  347.6 11.6 %scatter_custom_fusion.2 = f32[1024,256]{1,0:T(8,128)} fusion(s32[1536]{0:T(1024)S(1)} %fusion.14, f32[1536,256]{1,0:T(8,128)} %bitcast.49, f32[]{:T(128)} %constant.70.clone.1), kind=kCustom, calls=%fused_computation.20 | custom fusion | flops 393216 | bytes 1049088 | tf_op jit(solution)/shard_map/scatter-add | solution.py:94
  (27 shorter events, 0.3 us)
Async XLA Ops:
  7.2 29.3 %copy-start = (bf16[1024,256]{1,0:T(8,128)(2,1)S(1)}, bf16[1024,256]{1,0:T(8,128)(2,1)}, u32[]{:S(2)}) copy-start(bf16[1024,256]{1,0:T(8,128)(2,1)} %param.7) | copy-start | bytes 1572868
  42.4 31.5 %all-to-all-start.1 = ((bf16[12,128,256]{2,1,0:T(8,128)(2,1)}), bf16[12,128,256]{2,1,0:T(8,128)(2,1)S(1)}, u32[]{:S(2)}, u32[]{:S(2)}) async-start(bf16[12,128,256]{2,1,0:T(8,128)(2,1)} %broadcast_select_fusion), calls=%async_computation.1 | async-start | bytes 1572864 | tf_op jit(solution)/shard_map/all_to_all | solution.py:33
  46.1 29.9 %copy-start.1 = (bf16[256,1024]{1,0:T(8,128)(2,1)S(1)}, bf16[256,1024]{1,0:T(8,128)(2,1)}, u32[]{:S(2)}) copy-start(bf16[256,1024]{1,0:T(8,128)(2,1)} %param.8) | copy-start | bytes 1572868
  46.1 120.9 %all-gather.4.cloned.1.call-start = ((), (), s32[]{:S(2)}) async-start(), calls=%async_computation.3 | async-start | bytes 4259840 | tf_op jit(solution)/shard_map/all_gather | solution.py:49
  73.9 3.7 %copy-start.3 = (s32[3,32]{1,0:T(4,128)S(1)}, s32[3,32]{1,0:T(4,128)}, u32[]{:S(2)}) copy-start(s32[3,32]{1,0:T(4,128)} %param.12) | copy-start | bytes 1156
  73.9 61.6 %copy-start.2 = (bf16[32,1024]{1,0:T(8,128)(2,1)S(1)}, bf16[32,1024]{1,0:T(8,128)(2,1)}, u32[]{:S(2)}) copy-start(bf16[32,1024]{1,0:T(8,128)(2,1)} %param.10) | copy-start | bytes 196612
  73.9 61.6 %copy-start.4 = (s32[1,32]{1,0:T(1,128)S(1)}, s32[1,32]{1,0:T(1,128)}, u32[]{:S(2)}) copy-start(s32[1,32]{1,0:T(1,128)} %param.13) | copy-start | bytes 388
  76.8 192.4 %all-gather.6.cloned.1.call-start = ((), (), s32[]{:S(2)}) async-start(), calls=%async_computation.4 | async-start | bytes 12779520 | tf_op jit(solution)/shard_map/all_gather | solution.py:58
Sparse Core Ops, SparseCore 0:
  76.9 90.0 all-gather.3
  170.9 98.1 all-gather.5
where the time goes:
time: 367 us; the launch traced here: 366 us
  waiting for transfers between devices  157 us (43%)
  blocking collectives  148 us (40%)
  other arithmetic  16.1 us (4%)
  matrix products  14.3 us (4%)
  between operations  14.3 us (4%)
  local copies, waits for them, and re-layouts  12.4 us (3%)
  starting transfers between devices  3.74 us (1%)
    all_gather x1, waiting for transfers between devices, body(): stale_rows = lax.all_gather(memory, 'wide', axis=1, tiled=True)  98.3 us
    all_to_all x1, blocking collectives, body(): lax.all_to_all(outgoing, 'grp', split_axis=0, concat_axis=0, tiled=True)  66 us
    all_gather x1, blocking collectives, body(): slot_ages = lax.all_gather(slot_age, 'wide', axis=1, tiled=True)  57.5 us
    all_gather x1, waiting for transfers between devices, body(): lax.all_gather(items, 'wide', axis=0, tiled=True)  30.5 us
    all_to_all x1, waiting for transfers between devices, body(): lax.all_to_all(found, 'grp', split_axis=0, concat_axis=0, tiled=True)  27.7 us
    all_to_all x1, blocking collectives, body(): lax.all_to_all(requests, 'grp', split_axis=0, concat_axis=0, tiled=True)  24.4 us
    scatter-add x1, other arithmetic, body(): table_grad = jnp.zeros((rows_dev, emb_width), jnp.float32).at[targets].ad...  11.6 us
    dot_general x1, matrix products, body(): jnp.einsum('qd,snd->qsn', queries, stale_rows, preferred_element_type=jnp...  8.46 us
  transfers between devices with their start and end apart: 3, of which 3 were waited for; matrix products, arithmetic and copies ran while one was open for 1% of the time, Pallas kernels for 0%

commit v1 on v0

v1 whole, which is shorter than its diff:
```python
import math

import jax
import jax.numpy as jnp
from jax import lax
from jax.experimental import pallas as pl
from jax.experimental.pallas import tpu as pltpu
from jax.sharding import PartitionSpec as P

MESH = pl.DeviceIdType.MESH
NX, NY, NC, NZ = 4, 8, 2, 12
NQ = NY * NC
DEAD = -1e30
NT = (((1,), (1,)), ((), ()))
NN = (((1,), (0,)), ((), ()))
f32, bf16, i32 = jnp.float32, jnp.bfloat16, jnp.int32


def wrap(a, n):
    return jnp.where(a >= n, a - n, a)


def kernel(
    table, weight, meta, queries, memory,
    loss, grad,
    meta_z, meta_x, mem_x, yq, zq, psend, precv, pool_x, part, parts, coef_all,
    count, q4, items, pg_hi, pg_lo,
    ms, mr, xs, xr, es, er, ys, yr, cs, cr, zs, zr, ps, pr, os, orr, ls, lr, gs, gr,
):
    wide = lax.axis_index("wide")
    z = lax.axis_index("grp")
    y, x, c = wide // (NX * NC), (wide // NC) % NX, wide % NC
    q = c * NY + y
    factor = 2.0 / math.sqrt(queries.shape[1])
    base = (wide * NZ + z) * table.shape[0]
    rows = table.shape[0]
    nb = queries.shape[0]

    def dev(y_, x_, c_, z_):
        return ((y_ * NX + x_) * NC + c_, z_)

    def zdev(k):
        return dev(y, x, c, wrap(z + k, NZ))

    def xdev(k):
        return dev(y, (x + k) % NX, c, z)

    def ydev(k):
        return dev((y + k) % NY, x, c, z)

    def qdev(k):
        qq = (q + k) % NQ
        return dev(qq % NY, x, qq // NY, z)

    def rc(src, dst, s, r, to):
        return pltpu.make_async_remote_copy(src, dst, s, r, device_id=to, device_id_type=MESH)

    def loop(lo, hi, body):
        lax.fori_loop(lo, hi, lambda k, t: (body(k), t)[1], 0)

    barrier = pltpu.get_barrier_semaphore()

    def greet(to):
        pl.semaphore_signal(barrier, inc=1, device_id=to, device_id_type=MESH)

    loop(1, NZ, lambda k: greet(zdev(k)))
    loop(1, NQ, lambda k: greet(qdev(k)))
    loop(1, NX, lambda k: greet(xdev(k)))

    meta_z[z] = meta[...]
    meta_x[x] = meta[...]
    zq[z] = queries[...]
    yq[c, y] = queries[...]
    mem_x[x] = memory[...]
    for j in range(4):
        q4[j] = queries[...]
    pl.semaphore_wait(barrier, (NZ - 1) + (NQ - 1) + (NX - 1))

    def c_meta_z(k):
        return rc(meta, meta_z.at[z], ms.at[k], mr.at[k], zdev(k))

    def c_meta_x(k):
        return rc(meta, meta_x.at[x], xs.at[k], xr.at[k], xdev(k))

    def c_mem_x(k):
        return rc(memory, mem_x.at[x], es.at[k], er.at[k], xdev(k))

    def c_q_y(k):
        return rc(queries, yq.at[c, y], ys.at[k], yr.at[k], ydev(k))

    def c_q_c():
        return rc(yq.at[c], yq.at[c], cs, cr, dev(y, x, 1 - c, z))

    def c_ring(d, s):
        owner = wrap(z + s, NZ) if d == 0 else wrap(z - s + NZ, NZ)
        to = zdev(NZ - 1) if d == 0 else zdev(1)
        return rc(zq.at[owner], zq.at[owner], zs.at[d, s], zr.at[d, s], to)

    def ring_start(s):
        if s > 0:
            c_ring(0, s - 1).wait_recv()
            c_ring(1, s - 1).wait_recv()
        c_ring(0, s).start()
        if s < NZ // 2 - 1:
            c_ring(1, s).start()

    def c_part(k):
        return rc(psend.at[k], precv.at[z], ps.at[k], pr.at[k], zdev(k))

    def c_pool(k):
        return rc(pool_x.at[x], pool_x.at[x], os.at[k], orr.at[k], xdev(k))

    def c_lse(k):
        return rc(part.at[((q + k) % NQ) // 4], parts.at[q], ls.at[k], lr.at[k], qdev(k))

    def c_coef(k):
        return rc(coef_all.at[z], coef_all.at[z], gs.at[k], gr.at[k], zdev(k))

    loop(1, NZ, lambda k: c_meta_z(k).start())
    ring_start(0)
    loop(1, NX, lambda k: c_meta_x(k).start())
    loop(1, NX, lambda k: c_mem_x(k).start())
    loop(1, NY, lambda k: c_q_y(k).start())

    def partial_sums(owner):
        cols = jnp.transpose(meta_z[owner] - base)
        spots = lax.broadcasted_iota(i32, (nb, rows), 1)
        found = jnp.zeros((nb, rows), f32)
        for r in range(4):
            for b in range(4):
                col = cols[b * nb : (b + 1) * nb, r : r + 1]
                found = found + jnp.where(col == spots, 1.0, 0.0)
        return lax.dot_general(found.astype(bf16), table[...], NN, preferred_element_type=f32)

    loop(1, NZ, lambda k: c_meta_z(k).wait_recv())
    ring_start(1)

    def lookup(j):
        k = 6 + (1 - 2 * (j % 2)) * ((j + 1) // 2)
        psend[k] = partial_sums(wrap(z + k, NZ))
        c_part(k).start()

    loop(0, 4, lookup)
    ring_start(2)
    loop(4, NZ - 1, lookup)
    precv[z] = partial_sums(z)
    ring_start(3)

    loop(1, NY, lambda k: c_q_y(k).wait_recv())
    c_q_c().start()

    lane = lax.broadcasted_iota(i32, (8, 128), 1) // nb

    def counts(g):
        ids = []
        for b in range(4):
            lined = jnp.zeros((8, 128), i32)
            for d in range(4):
                rolled = meta_z[4 * g + d] - base
                if d != b:
                    rolled = pltpu.roll(rolled, ((d - b) * nb) % 128, 1)
                lined = jnp.where(lane == d, rolled, lined)
            ids.append(lined)
        step = 128

        def block(t):
            spots = lax.broadcasted_iota(i32, (step, 128), 0) + t * step
            found = jnp.zeros((step, 128), f32)
            for b in range(4):
                for r in range(4):
                    found = found + jnp.where(ids[b][r : r + 1, :] == spots, 1.0, 0.0)
            count[g, pl.ds(pl.multiple_of(t * step, step), step), :] = found.astype(bf16)

        loop(0, rows // step, block)

    for g in range(3):
        counts(g)
    ring_start(4)

    loop(1, NX, lambda k: c_meta_x(k).wait_recv())
    loop(1, NX, lambda k: c_mem_x(k).wait_recv())
    c_q_c().wait_recv()
    all_q = yq[...].reshape(NQ * nb, queries.shape[1])

    high = jnp.full((1, NQ * nb), DEAD, f32)
    total = jnp.zeros((1, NQ * nb), f32)

    def stale(t, carry):
        high, total = carry
        keys = mem_x[t].reshape(3 * nb, queries.shape[1])
        score = lax.dot_general(keys, all_q, NT, preferred_element_type=f32) * factor
        ages = jnp.transpose(meta_x[t])
        age = jnp.concatenate([ages[0:nb, 5 + s : 6 + s] for s in range(3)], axis=0)
        score = jnp.where(age <= 3, score, DEAD)
        new = jnp.maximum(high, jnp.max(score, axis=0, keepdims=True))
        total = total * jnp.exp(high - new) + jnp.sum(jnp.exp(score - new), axis=0, keepdims=True)
        return new, total

    high, total = lax.fori_loop(0, NX, stale, (high, total))

    loop(1, NZ, lambda k: c_part(k).wait_recv())
    pooled = precv[0]
    for s in range(1, NZ):
        pooled = pooled + precv[s]
    pool_x[x] = (pooled / 16.0).astype(bf16)
    loop(1, NX, lambda k: c_pool(k).start())
    ring_start(5)
    loop(1, NX, lambda k: c_pool(k).wait_recv())
    every = pool_x[...].reshape(NX * nb, table.shape[1])
    items[...] = lax.dot_general(every, weight[...], NN, preferred_element_type=f32).astype(bf16)

    score = lax.dot_general(items[...], all_q, NT, preferred_element_type=f32) * factor
    new = jnp.maximum(high, jnp.max(score, axis=0, keepdims=True))
    total = total * jnp.exp(high - new) + jnp.sum(jnp.exp(score - new), axis=0, keepdims=True)
    for g in range(4):
        part[g, 0:1, :] = new[:, 128 * g : 128 * (g + 1)]
        part[g, 1:2, :] = total[:, 128 * g : 128 * (g + 1)]
    parts[q] = part[q // 4]
    loop(1, NQ, lambda k: c_lse(k).start())

    mine = items[pl.ds(pl.multiple_of(x * nb, nb), nb), :]
    own = lax.dot_general(
        mine, q4[...].reshape(4 * nb, queries.shape[1]), NT, preferred_element_type=f32
    ) * factor
    chosen = meta[4:5, :] == lax.broadcasted_iota(i32, (nb, 128), 0)
    hit = jnp.sum(jnp.where(chosen, own, 0.0), axis=0, keepdims=True)
    lanes = lax.broadcasted_iota(i32, (nb, 128), 1) // nb

    loop(1, NQ, lambda k: c_lse(k).wait_recv())
    got = parts[...]
    highs, totals = got[:, 0, :], got[:, 1, :]
    top = jnp.max(highs, axis=0, keepdims=True)
    lse = top + jnp.log(jnp.sum(totals * jnp.exp(highs - top), axis=0, keepdims=True))
    lse = jnp.where(lanes[0:1] == q % 4, lse, 0.0)
    lse = lse + pltpu.roll(lse, 64, 1)
    lse = lse + pltpu.roll(lse, 32, 1)
    loss[...] = lse - hit
    coef = jnp.exp(own - lse) - jnp.where(chosen, 1.0, 0.0)
    coef_all[z] = jnp.where(lanes == z % 4, coef, 0.0).astype(bf16)
    loop(1, NZ, lambda k: c_coef(k).start())

    c_ring(0, NZ // 2 - 1).wait_recv()
    loop(1, NZ, lambda k: c_coef(k).wait_recv())
    for g in range(3):
        held = coef_all[4 * g : 4 * g + 4].reshape(4 * nb, 128)
        asked = zq[4 * g : 4 * g + 4].reshape(4 * nb, queries.shape[1])
        item_grad = (
            lax.dot_general(held, asked, NN, preferred_element_type=f32) * factor
        ).astype(bf16)
        pooled_grad = lax.dot_general(item_grad, weight[...], NT, preferred_element_type=f32) / 16.0
        upper = pooled_grad.astype(bf16)
        pg_hi[g] = upper
        pg_lo[g] = (pooled_grad - upper.astype(f32)).astype(bf16)

    def spread(t):
        step = 256
        spot = pl.ds(pl.multiple_of(t * step, step), step)
        out = jnp.zeros((step, table.shape[1]), f32)
        for g in range(3):
            found = count[g, spot, :]
            out = out + lax.dot_general(found, pg_hi[g], NN, preferred_element_type=f32)
            out = out + lax.dot_general(found, pg_lo[g], NN, preferred_element_type=f32)
        grad[spot, :] = out

    loop(0, rows // 256, spread)

    loop(1, NZ, lambda k: c_meta_z(k).wait_send())
    loop(1, NX, lambda k: c_meta_x(k).wait_send())
    loop(1, NX, lambda k: c_mem_x(k).wait_send())
    loop(1, NY, lambda k: c_q_y(k).wait_send())
    c_q_c().wait_send()
    for s in range(NZ // 2):
        c_ring(0, s).wait_send()
        if s < NZ // 2 - 1:
            c_ring(1, s).wait_send()
    loop(1, NZ, lambda k: c_part(k).wait_send())
    loop(1, NX, lambda k: c_pool(k).wait_send())
    loop(1, NQ, lambda k: c_lse(k).wait_send())
    loop(1, NZ, lambda k: c_coef(k).wait_send())


def body(table, item_weight, ids, queries, memory, slot_age, positive):
    nb, dim = queries.shape
    rows, emb = table.shape
    meta = jnp.concatenate(
        [
            ids.reshape(nb, 16).T.reshape(4, 4 * nb),
            jnp.tile(positive, (1, 4)),
            jnp.tile(slot_age, (1, 4)),
        ],
        axis=0,
    )
    vmem = pl.BlockSpec(memory_space=pltpu.VMEM)
    dma = pltpu.SemaphoreType.DMA
    loss, grad = pl.pallas_call(
        kernel,
        out_shape=(
            jax.ShapeDtypeStruct((1, 128), f32),
            jax.ShapeDtypeStruct((rows, emb), f32),
        ),
        in_specs=[vmem] * 5,
        out_specs=(vmem, vmem),
        scratch_shapes=[
            pltpu.VMEM((NZ, 8, 128), i32),
            pltpu.VMEM((NX, 8, 128), i32),
            pltpu.VMEM((NX, 3, nb, dim), bf16),
            pltpu.VMEM((NC, NY, nb, dim), bf16),
            pltpu.VMEM((NZ, nb, dim), bf16),
            pltpu.VMEM((NZ, nb, emb), f32),
            pltpu.VMEM((NZ, nb, emb), f32),
            pltpu.VMEM((NX, nb, emb), bf16),
            pltpu.VMEM((4, 8, 128), f32),
            pltpu.VMEM((NQ, 8, 128), f32),
            pltpu.VMEM((NZ, nb, 128), bf16),
            pltpu.VMEM((3, rows, 128), bf16),
            pltpu.VMEM((4, nb, dim), bf16),
            pltpu.VMEM((NX * nb, dim), bf16),
            pltpu.VMEM((3, 128, emb), bf16),
            pltpu.VMEM((3, 128, emb), bf16),
            dma((NZ,)), dma((NZ,)),
            dma((NX,)), dma((NX,)),
            dma((NX,)), dma((NX,)),
            dma((NY,)), dma((NY,)),
            dma, dma,
            dma((2, NZ // 2)), dma((2, NZ // 2)),
            dma((NZ,)), dma((NZ,)),
            dma((NX,)), dma((NX,)),
            dma((NQ,)), dma((NQ,)),
            dma((NZ,)), dma((NZ,)),
        ],
        compiler_params=pltpu.CompilerParams(
            collective_id=0, has_side_effects=True, vmem_limit_bytes=40 * 1024 * 1024
        ),
        name="step",
    )(table, item_weight, meta, queries, memory)
    return loss[0, :nb], grad


def solution(mesh):
    split = P(("wide", "grp"))
    rows = P(("wide", "grp"), None)
    return jax.shard_map(
        body,
        mesh=mesh,
        in_specs=(
            rows, P(), split, rows, P(None, ("wide", "grp"), None), P(None, ("wide", "grp")), rows,
        ),
        out_specs=(split, rows),
        check_vma=False,
    )
```

time: 367 us -> 74.1 us (0.20)
  waiting for transfers between devices: 157 us -> 0 us
  blocking collectives: 148 us -> 0 us
  Pallas kernels: 0 us -> 66.2 us
  other arithmetic: 16.1 us -> 0.01 us
  matrix products: 14.3 us -> 0 us
  between operations: 14.3 us -> 0.68 us
  local copies, waits for them, and re-layouts: 12.4 us -> 6.89 us
  starting transfers between devices: 3.74 us -> 0 us
    all_gather x2 -> x0, waiting for transfers between devices: 129 us -> none  [the longest x1 98.3 us: body(): stale_rows = lax.all_gather(memory, 'wide', axis=1, tiled=True)]
    all_to_all x2 -> x0, blocking collectives: 90.5 us -> none  [the longest x1 66 us: body(): lax.all_to_all(outgoing, 'grp', split_axis=0, concat_axis=0, tiled=True)]
    pallas_call x0 -> x1, Pallas kernels: none -> 66.2 us  [body(): pl.pallas_call(kernel, out_shape=(jax.ShapeDtypeStruct((1, 128), f32), ja...]
    all_gather x1 -> x0, blocking collectives: 57.5 us -> none  [body(): slot_ages = lax.all_gather(slot_age, 'wide', axis=1, tiled=True)]
    all_to_all x1 -> x0, waiting for transfers between devices: 27.7 us -> none  [body(): lax.all_to_all(found, 'grp', split_axis=0, concat_axis=0, tiled=True)]
    dot_general x5 -> x0, matrix products: 14.3 us -> none  [the longest x1 8.46 us: body(): jnp.einsum('qd,snd->qsn', queries, stale_rows, preferred_element_type=jnp...]
    scatter-add x1 -> x0, other arithmetic: 11.6 us -> none  [body(): table_grad = jnp.zeros((rows_dev, emb_width), jnp.float32).at[targets].ad...]
    gather x2 -> x0, local copies, waits for them, and re-layouts: 6.71 us -> none  [the longest x1 4.76 us: body(): found = table[jnp.maximum(asked, 0)]]
  transfers between devices with their start and end apart: 3 -> 0, of which waited for: 3 -> 0; matrix products, arithmetic and copies ran while one was open for 1% -> 0% of each run, Pallas kernels for 0% -> 0%
where the time goes in v1:
time: 74.1 us; the launch traced here: 73.8 us
  Pallas kernels  66.2 us (89%)
  local copies, waits for them, and re-layouts  6.89 us (9%)
    pallas_call x1, Pallas kernels, body(): pl.pallas_call(kernel, out_shape=(jax.ShapeDtypeStruct((1, 128), f32), ja...  66.2 us
    unnamed x11, local copies, waits for them, and re-layouts  4.62 us

profile of v1, /device:TPU:1, one launch (start us, length us, event | category | flops | bytes accessed | tf_op | source)
XLA Modules:
  0.0 73.8 jit_solution(5934409698477739206)
XLA Ops:
  0.6 0.0 copy-start.4
  0.6 0.0 copy-start.3
  0.6 0.6 copy-done.4
  1.3 0.1 tile.22
  1.4 0.7 tile.23
  2.1 0.1 tile.24
  2.1 0.8 %reshape.20 = s32[32,16]{1,0:T(8,128)S(1)} reshape(s32[512]{0:T(512)} %param.9) | data formatting | bytes 4096 | tf_op jit(solution)/shard_map/reshape | solution.py:287
  2.9 0.1 copy.9
  3.0 0.1 reshape.21
  3.1 0.0 copy-done.3
  3.1 0.0 copy-start
  3.1 1.0 %copy-done = bf16[1024,256]{1,0:T(8,128)(2,1)S(1)} copy-done((bf16[1024,256]{1,0:T(8,128)(2,1)S(1)}, bf16[1024,256]{1,0:T(8,128)(2,1)}, u32[]{:S(2)}) %copy-start) | copy-done | bytes 524312
  4.1 0.0 copy-start.1
  4.1 1.0 %copy-done.1 = bf16[256,1024]{1,0:T(8,128)(2,1)S(1)} copy-done((bf16[256,1024]{1,0:T(8,128)(2,1)S(1)}, bf16[256,1024]{1,0:T(8,128)(2,1)}, u32[]{:S(2)}) %copy-start.1) | copy-done | bytes 524312
  5.2 0.0 copy-start.2
  5.2 0.9 %copy-done.2 = bf16[3,32,1024]{2,1,0:T(8,128)(2,1)S(1)} copy-done((bf16[3,32,1024]{2,1,0:T(8,128)(2,1)S(1)}, bf16[3,32,1024]{2,1,0:T(8,128)(2,1)}, u32[]{:S(2)}) %copy-start.2) | copy-done | bytes 196632
  6.1 66.2 %step.1 = (f32[1,128]{1,0:T(1,128)S(1)}, f32[1024,256]{1,0:T(8,128)S(1)}) custom-call(bf16[1024,256]{1,0:T(8,128)(2,1)S(1)} %copy-done, bf16[256,1024]{1,0:T(8,128)(2,1)S(1)} %copy-done.1, s32[8,128]{1,0:T(8,128)S(1)} %pad_add_fusion.meta, bf16[32,1024]{1,0:T(8,128)(2,1)S(1)} %copy-done.3, bf16[3,32,1024]{2,1,0:T(8,128)(2,1)S(1)} %copy-done.2), custom_call_target="tpu_custom_call" | custom-call | tf_op jit(solution)/shard_map/step/pallas_call | solution.py:295
  72.3 0.5 slice_bitcast_fusion
  72.8 1.0 %copy.11 = f32[1024,256]{1,0:T(8,128)} copy(f32[1024,256]{1,0:T(8,128)S(1)} %get-tuple-element.9) | data formatting | bytes 2097152
  (2 shorter events, 0.0 us)
Async XLA Ops:
  0.6 0.7 copy-start.4
  0.6 2.4 %copy-start.3 = (bf16[32,1024]{1,0:T(8,128)(2,1)S(1)}, bf16[32,1024]{1,0:T(8,128)(2,1)}, u32[]{:S(2)}) copy-start(bf16[32,1024]{1,0:T(8,128)(2,1)} %queries.1) | copy-start | bytes 196612
  3.1 1.0 %copy-start = (bf16[1024,256]{1,0:T(8,128)(2,1)S(1)}, bf16[1024,256]{1,0:T(8,128)(2,1)}, u32[]{:S(2)}) copy-start(bf16[1024,256]{1,0:T(8,128)(2,1)} %table.1) | copy-start | bytes 1572868
  4.1 1.0 %copy-start.1 = (bf16[256,1024]{1,0:T(8,128)(2,1)S(1)}, bf16[256,1024]{1,0:T(8,128)(2,1)}, u32[]{:S(2)}) copy-start(bf16[256,1024]{1,0:T(8,128)(2,1)} %weight.1) | copy-start | bytes 1572868
  5.2 0.9 %copy-start.2 = (bf16[3,32,1024]{2,1,0:T(8,128)(2,1)S(1)}, bf16[3,32,1024]{2,1,0:T(8,128)(2,1)}, u32[]{:S(2)}) copy-start(bf16[3,32,1024]{2,1,0:T(8,128)(2,1)} %memory.1) | copy-start | bytes 589828

commit v2 on v1

v2 whole, which is shorter than its diff:
```python
import math

import jax
import jax.numpy as jnp
from jax import lax
from jax.experimental import pallas as pl
from jax.experimental.pallas import tpu as pltpu
from jax.sharding import PartitionSpec as P

MESH = pl.DeviceIdType.MESH
NX, NY, NC, NZ = 4, 8, 2, 12
NQ = NY * NC
DEAD = -1e30
NT = (((1,), (1,)), ((), ()))
NN = (((1,), (0,)), ((), ()))
f32, bf16, i32 = jnp.float32, jnp.bfloat16, jnp.int32


def wrap(a, n):
    return jnp.where(a >= n, a - n, a)


class Copies:
    def __init__(self, make, ks):
        self.make, self.ks = make, ks

    def each(self, act):
        if isinstance(self.ks, range):
            lax.fori_loop(self.ks[0], self.ks[-1] + 1, lambda k, t: (act(self.make(k)), t)[1], 0)
        else:
            for k in self.ks:
                act(self.make(k))

    def only(self, *ks):
        return Copies(self.make, ks)

    def start(self):
        self.each(lambda copy: copy.start())

    def recv(self):
        self.each(lambda copy: copy.wait_recv())

    def sent(self):
        self.each(lambda copy: copy.wait_send())


def kernel(
    table_hbm, weight_hbm, ids_hbm, queries_hbm, memory_hbm, ages_hbm, positive_hbm,
    loss, grad,
    table, weight, ids, label, ages, meta, marks, cols,
    meta_z, meta_x, mem_x, yq, zq, psend, precv, relayed, pool_x, part, parts, coef_all,
    count, q4, items, pg_hi, pg_lo,
    ds, ms, mr, xs, xr, es, er, hs, hr, ys, yr, cs, cr, zs, zr, ps, pr, rs, rr, os, orr, ls, lr, gs, gr,
):
    wide = lax.axis_index("wide")
    z = lax.axis_index("grp")
    y, x, c = wide // (NX * NC), (wide // NC) % NX, wide % NC
    q = c * NY + y
    nb, dim = queries_hbm.shape
    factor = 2.0 / math.sqrt(dim)
    rows, emb = table_hbm.shape
    base = (wide * NZ + z) * rows

    def dev(y_, x_, c_, z_):
        return ((y_ * NX + x_) * NC + c_, z_)

    def zdev(k):
        return dev(y, x, c, wrap(z + k, NZ))

    def xdev(k):
        return dev(y, (x + k) % NX, c, z)

    def ydev(k):
        return dev((y + k) % NY, x, c, z)

    def qdev(k):
        qq = (q + k) % NQ
        return dev(qq % NY, x, qq // NY, z)

    def rc(src, dst, s, r, to):
        return pltpu.make_async_remote_copy(src, dst, s, r, device_id=to, device_id_type=MESH)

    def loop(lo, hi, body):
        lax.fori_loop(lo, hi, lambda k, t: (body(k), t)[1], 0)

    opened = []

    def start(*kinds):
        for kind in kinds:
            kind.start()
            opened.append(kind)

    def recv(*kinds):
        for kind in kinds:
            kind.recv()

    loads = [
        pltpu.make_async_copy(src, dst, ds.at[n])
        for n, (src, dst) in enumerate(
            [(ids_hbm, ids.at[0:4]), (positive_hbm, label), (ages_hbm, ages), (memory_hbm, mem_x.at[x])]
            + [(queries_hbm, dst) for dst in [yq.at[c, y], zq.at[z]] + [q4.at[j] for j in range(4)]]
            + [(table_hbm, table), (weight_hbm, weight)]
        )
    ]
    for load in loads:
        load.start()

    barrier = pltpu.get_barrier_semaphore()

    def greet(to):
        pl.semaphore_signal(barrier, inc=1, device_id=to, device_id_type=MESH)

    loop(1, NZ, lambda k: greet(zdev(k)))
    loop(1, NQ, lambda k: greet(qdev(k)))
    loop(1, NX, lambda k: greet(xdev(k)))

    ids[4:8] = jnp.zeros((4, 128), i32)
    marks[...] = jnp.zeros((8, 128), i32)
    for load in loads[:3]:
        load.wait()
    cols[...] = jnp.transpose(ids[...])
    marks[4:5, 0:nb] = label[...]
    marks[5:8, 0:nb] = ages[...]
    spot = lax.broadcasted_iota(i32, (8, 8), 1)
    byte = [cols[pl.ds(b, 8, stride=16), :] for b in range(16)]
    lines = []
    for b in range(4):
        for r in range(4):
            line = jnp.zeros((8, 8), i32)
            for t in range(4):
                line = jnp.where(spot == t, byte[4 * t + b][:, r : r + 1], line)
            lines.append(line)
    lined = jnp.transpose(jnp.concatenate(lines, axis=0))
    marked = marks[...]
    marked = marked + pltpu.roll(marked, 32, 1)
    marked = marked + pltpu.roll(marked, 64, 1)
    own_meta = jnp.where(lax.broadcasted_iota(i32, (8, 128), 0) < 4, lined, marked)
    meta[...] = own_meta
    meta_z[z] = own_meta
    meta_x[x] = own_meta
    for load in loads[3:10]:
        load.wait()
    pl.semaphore_wait(barrier, (NZ - 1) + (NQ - 1) + (NX - 1))

    def ring(s, d):
        owner = wrap(z + s, NZ) if d == 0 else wrap(z - s + NZ, NZ)
        to = zdev(NZ - 1) if d == 0 else zdev(1)
        return rc(zq.at[owner], zq.at[owner], zs.at[d, s], zr.at[d, s], to)

    def half(r):
        block = mem_x.at[(x + 1 + 2 * r) % NX, :, nb // 2 * r : nb // 2 * (r + 1)]
        return rc(block, block, hs.at[r], hr.at[r], xdev(3 - 2 * r))

    def fourth(_):
        block = yq.at[c, (y + 3) % NY]
        return rc(block, block, ys.at[4], yr.at[4], ydev(NY - 1))

    def across(k):
        block = yq.at[c, (y - k + NY) % NY]
        return rc(block, block, cs.at[k], cr.at[k], dev(y, x, 1 - c, z))

    def relay(j):
        to = zdev(jnp.where(j == 2, NZ - 1, 2 - j))
        return rc(psend.at[far(j)], relayed.at[j], rs.at[j], rr.at[j], to)

    def far(j):
        return 6 + (1 - 2 * (j % 2)) * ((j + 1) // 2)

    def near(j):
        d = 3 - j // 2
        return jnp.where(j % 2 == 0, d, NZ - d)

    c_meta_z = Copies(lambda k: rc(meta, meta_z.at[z], ms.at[k], mr.at[k], zdev(k)), range(1, NZ))
    c_meta_x = Copies(lambda k: rc(meta, meta_x.at[x], xs.at[k], xr.at[k], xdev(k)), range(1, NX))
    c_mem_x = Copies(lambda k: rc(mem_x.at[x], mem_x.at[x], es.at[k], er.at[k], xdev(k)), (1, 3))
    c_half = Copies(half, (0, 1))
    c_q_y = Copies(
        lambda k: rc(yq.at[c, y], yq.at[c, y], ys.at[k], yr.at[k], ydev(k)), (5, 3, 6, 2, 7, 1)
    )
    c_fourth = Copies(fourth, (4,))
    c_across = Copies(across, range(0, NY))
    c_ring = [
        Copies(lambda d, s=s: ring(s, d), (0, 1) if s < NZ // 2 - 1 else (0,)) for s in range(NZ // 2)
    ]
    c_relay = Copies(relay, range(0, 3))
    c_part = Copies(
        lambda k: rc(psend.at[k], precv.at[k], ps.at[k], pr.at[k], zdev(k)), (1, 11, 2, 10, 3, 9, 4, 8)
    )
    c_pool = Copies(
        lambda k: rc(pool_x.at[x], pool_x.at[x], os.at[k], orr.at[k], xdev(k)), (2, 1, 3)
    )
    c_lse = Copies(
        lambda k: rc(part.at[((q + k) % NQ) // 4], parts.at[q], ls.at[k], lr.at[k], qdev(k)),
        range(1, NQ),
    )
    c_coef = Copies(
        lambda k: rc(coef_all.at[z], coef_all.at[z], gs.at[k], gr.at[k], zdev(k)), range(1, NZ)
    )

    def ring_start(s):
        if s > 0:
            recv(c_ring[s - 1])
        start(c_ring[s])

    start(c_meta_z, c_meta_x, c_mem_x, c_q_y, c_across.only(0))

    def partial_sums(owner):
        wanted = jnp.transpose(meta_z[owner] - base)
        spots = lax.broadcasted_iota(i32, (nb, rows), 1)
        found = jnp.zeros((nb, rows), f32)
        for r in range(4):
            for b in range(4):
                col = wanted[b * nb : (b + 1) * nb, r : r + 1]
                found = found + jnp.where(col == spots, 1.0, 0.0)
        return lax.dot_general(found.astype(bf16), table[...], NN, preferred_element_type=f32)

    recv(c_meta_z.only(3, 9, 2, 10, 1, 11))
    ring_start(0)
    for load in loads[10:]:
        load.wait()

    def lookup_near(j):
        k = near(j)
        psend[k] = partial_sums(wrap(z + k, NZ))
        c_part.make(k).start()

    def lookup_far(j):
        k = far(j)
        psend[k] = partial_sums(wrap(z + k, NZ))
        relay(j).start()

    def lookup_fourth(j):
        k = far(j)
        psend[k] = partial_sums(wrap(z + k, NZ))

    loop(0, 6, lookup_near)
    recv(c_meta_z.only(6, 5, 7, 4, 8))
    loop(0, 3, lookup_far)
    recv(c_mem_x)
    start(c_half)
    loop(3, 5, lookup_fourth)
    precv[0] = partial_sums(z)
    recv(c_relay)
    psend[4] = psend[4] + (relayed[0] + relayed[1])
    psend[8] = psend[8] + relayed[2]
    start(c_part.only(4, 8))
    opened.extend([c_part.only(1, 11, 2, 10, 3, 9), c_relay])
    ring_start(1)

    recv(c_q_y.only(5))
    start(c_fourth)
    for k in (7, 1, 6, 2, 5, 3):
        if k != 5:
            recv(c_q_y.only(k))
        start(c_across.only(k))

    recv(c_part)
    pooled = precv[0]
    for k in (1, 11, 2, 10, 3, 9, 4, 8):
        pooled = pooled + precv[k]
    pool_x[x] = (pooled / 16.0).astype(bf16)
    start(c_pool)
    recv(c_fourth)
    start(c_across.only(4))
    ring_start(2)

    recv(c_meta_x, c_half, c_across)
    all_q = yq[...].reshape(NQ * nb, dim)

    high = jnp.full((1, NQ * nb), DEAD, f32)
    total = jnp.zeros((1, NQ * nb), f32)

    def stale(t, carry):
        high, total = carry
        keys = mem_x[t].reshape(3 * nb, dim)
        score = lax.dot_general(keys, all_q, NT, preferred_element_type=f32) * factor
        marked = jnp.transpose(meta_x[t])
        age = jnp.concatenate([marked[0:nb, 5 + s : 6 + s] for s in range(3)], axis=0)
        score = jnp.where(age <= 3, score, DEAD)
        new = jnp.maximum(high, jnp.max(score, axis=0, keepdims=True))
        total = total * jnp.exp(high - new) + jnp.sum(jnp.exp(score - new), axis=0, keepdims=True)
        return new, total

    high, total = lax.fori_loop(0, NX, stale, (high, total))

    recv(c_pool)
    every = pool_x[...].reshape(NX * nb, emb)
    items[...] = lax.dot_general(every, weight[...], NN, preferred_element_type=f32).astype(bf16)

    score = lax.dot_general(items[...], all_q, NT, preferred_element_type=f32) * factor
    new = jnp.maximum(high, jnp.max(score, axis=0, keepdims=True))
    total = total * jnp.exp(high - new) + jnp.sum(jnp.exp(score - new), axis=0, keepdims=True)
    for g in range(4):
        part[g, 0:1, :] = new[:, 128 * g : 128 * (g + 1)]
        part[g, 1:2, :] = total[:, 128 * g : 128 * (g + 1)]
    parts[q] = part[q // 4]
    start(c_lse)
    ring_start(3)

    mine = items[pl.ds(pl.multiple_of(x * nb, nb), nb), :]
    own = lax.dot_general(
        mine, q4[...].reshape(4 * nb, dim), NT, preferred_element_type=f32
    ) * factor
    chosen = meta[4:5, :] == lax.broadcasted_iota(i32, (nb, 128), 0)
    hit = jnp.sum(jnp.where(chosen, own, 0.0), axis=0, keepdims=True)
    lanes = lax.broadcasted_iota(i32, (nb, 128), 1) // nb

    lane = lax.broadcasted_iota(i32, (8, 128), 1) // nb

    def counts(g):
        ids = []
        for b in range(4):
            lined = jnp.zeros((8, 128), i32)
            for d in range(4):
                rolled = meta_z[4 * g + d] - base
                if d != b:
                    rolled = pltpu.roll(rolled, ((d - b) * nb) % 128, 1)
                lined = jnp.where(lane == d, rolled, lined)
            ids.append(lined)
        step = 128

        def block(t):
            spots = lax.broadcasted_iota(i32, (step, 128), 0) + t * step
            found = jnp.zeros((step, 128), f32)
            for b in range(4):
                for r in range(4):
                    found = found + jnp.where(ids[b][r : r + 1, :] == spots, 1.0, 0.0)
            count[g, pl.ds(pl.multiple_of(t * step, step), step), :] = found.astype(bf16)

        loop(0, rows // step, block)

    counts(0)
    ring_start(4)
    recv(c_lse)
    got = parts[...]
    highs, totals = got[:, 0, :], got[:, 1, :]
    top = jnp.max(highs, axis=0, keepdims=True)
    lse = top + jnp.log(jnp.sum(totals * jnp.exp(highs - top), axis=0, keepdims=True))
    lse = jnp.where(lanes[0:1] == q % 4, lse, 0.0)
    lse = lse + pltpu.roll(lse, 64, 1)
    lse = lse + pltpu.roll(lse, 32, 1)
    loss[...] = lse - hit
    coef = jnp.exp(own - lse) - jnp.where(chosen, 1.0, 0.0)
    coef_all[z] = jnp.where(lanes == z % 4, coef, 0.0).astype(bf16)
    start(c_coef)
    ring_start(5)
    counts(1)
    counts(2)

    recv(c_ring[NZ // 2 - 1], c_coef)
    for g in range(3):
        held = coef_all[4 * g : 4 * g + 4].reshape(4 * nb, 128)
        asked = zq[4 * g : 4 * g + 4].reshape(4 * nb, dim)
        item_grad = (
            lax.dot_general(held, asked, NN, preferred_element_type=f32) * factor
        ).astype(bf16)
        pooled_grad = lax.dot_general(item_grad, weight[...], NT, preferred_element_type=f32) / 16.0
        upper = pooled_grad.astype(bf16)
        pg_hi[g] = upper
        pg_lo[g] = (pooled_grad - upper.astype(f32)).astype(bf16)

    def spread(t):
        step = 256
        spot = pl.ds(pl.multiple_of(t * step, step), step)
        out = jnp.zeros((step, emb), f32)
        for g in range(3):
            found = count[g, spot, :]
            out = out + lax.dot_general(found, pg_hi[g], NN, preferred_element_type=f32)
            out = out + lax.dot_general(found, pg_lo[g], NN, preferred_element_type=f32)
        grad[spot, :] = out

    loop(0, rows // 256, spread)

    for kind in opened:
        kind.sent()


def body(table, item_weight, ids, queries, memory, slot_age, positive):
    nb, dim = queries.shape
    rows, emb = table.shape
    arguments = (table, item_weight, ids.reshape(4, 4 * nb), queries, memory, slot_age, positive)
    vmem = pl.BlockSpec(memory_space=pltpu.VMEM)
    dma = pltpu.SemaphoreType.DMA
    loss, grad = pl.pallas_call(
        kernel,
        out_shape=(
            jax.ShapeDtypeStruct((1, 128), f32),
            jax.ShapeDtypeStruct((rows, emb), f32),
        ),
        in_specs=[pl.BlockSpec(memory_space=pltpu.HBM)] * 7,
        out_specs=(vmem, vmem),
        scratch_shapes=[
            pltpu.VMEM((rows, emb), bf16),
            pltpu.VMEM((emb, dim), bf16),
            pltpu.VMEM((8, 128), i32),
            pltpu.VMEM((1, nb), i32),
            pltpu.VMEM((3, nb), i32),
            pltpu.VMEM((8, 128), i32),
            pltpu.VMEM((8, 128), i32),
            pltpu.VMEM((128, 8), i32),
            pltpu.VMEM((NZ, 8, 128), i32),
            pltpu.VMEM((NX, 8, 128), i32),
            pltpu.VMEM((NX, 3, nb, dim), bf16),
            pltpu.VMEM((NC, NY, nb, dim), bf16),
            pltpu.VMEM((NZ, nb, dim), bf16),
            pltpu.VMEM((NZ, nb, emb), f32),
            pltpu.VMEM((NZ, nb, emb), f32),
            pltpu.VMEM((3, nb, emb), f32),
            pltpu.VMEM((NX, nb, emb), bf16),
            pltpu.VMEM((4, 8, 128), f32),
            pltpu.VMEM((NQ, 8, 128), f32),
            pltpu.VMEM((NZ, nb, 128), bf16),
            pltpu.VMEM((3, rows, 128), bf16),
            pltpu.VMEM((4, nb, dim), bf16),
            pltpu.VMEM((NX * nb, dim), bf16),
            pltpu.VMEM((3, 128, emb), bf16),
            pltpu.VMEM((3, 128, emb), bf16),
            dma((12,)),
            dma((NZ,)), dma((NZ,)),
            dma((NX,)), dma((NX,)),
            dma((NX,)), dma((NX,)),
            dma((2,)), dma((2,)),
            dma((NY,)), dma((NY,)),
            dma((NY,)), dma((NY,)),
            dma((2, NZ // 2)), dma((2, NZ // 2)),
            dma((NZ,)), dma((NZ,)),
            dma((3,)), dma((3,)),
            dma((NX,)), dma((NX,)),
            dma((NQ,)), dma((NQ,)),
            dma((NZ,)), dma((NZ,)),
        ],
        compiler_params=pltpu.CompilerParams(
            collective_id=0, has_side_effects=True, vmem_limit_bytes=40 * 1024 * 1024
        ),
        name="step",
    )(*(pltpu.with_memory_space_constraint(a, pltpu.HBM) for a in arguments))
    return loss[0, :nb], grad


def solution(mesh):
    split = P(("wide", "grp"))
    rows = P(("wide", "grp"), None)
    return jax.shard_map(
        body,
        mesh=mesh,
        in_specs=(
            rows, P(), split, rows, P(None, ("wide", "grp"), None), P(None, ("wide", "grp")), rows,
        ),
        out_specs=(split, rows),
        check_vma=False,
    )
```

time: 74.1 us -> 62.6 us (0.84)
  Pallas kernels: 66.2 us -> 60.3 us
  local copies, waits for them, and re-layouts: 6.89 us -> 1.48 us
    pallas_call x1, Pallas kernels: 66.2 us -> 60.3 us  [body(): pl.pallas_call(kernel, out_shape=(jax.ShapeDtypeStruct((1, 128), f32), ja...]
    unnamed x11 -> x1, local copies, waits for them, and re-layouts: 4.62 us -> 0.97 us
    another operation x4 -> x0, local copies, waits for them, and re-layouts: 0.86 us -> none  [the longest x2 0.77 us: body(): jnp.tile(slot_age, (1, 4))]
    reshape x2 -> x0, local copies, waits for them, and re-layouts: 0.84 us -> none  [body(): ids.reshape(nb, 16).T.reshape(4, 4 * nb)]
where the time goes in v2:
time: 62.6 us; the launch traced here: 62.4 us
  Pallas kernels  60.3 us (96%)
  local copies, waits for them, and re-layouts  1.48 us (2%)
  between operations  0.64 us (1%)
    pallas_call x1, Pallas kernels, body(): pl.pallas_call(kernel, out_shape=(jax.ShapeDtypeStruct((1, 128), f32), ja...  60.3 us

profile of v2, /device:TPU:1, one launch (start us, length us, event | category | flops | bytes accessed | tf_op | source)
XLA Modules:
  0.0 62.4 jit_solution(2794336759706613290)
XLA Ops:
  0.6 60.3 %step.1 = (f32[1,128]{1,0:T(1,128)S(1)}, f32[1024,256]{1,0:T(8,128)S(1)}) custom-call(bf16[1024,256]{1,0:T(8,128)(2,1)} %table_hbm.1, bf16[256,1024]{1,0:T(8,128)(2,1)} %weight_hbm.1, s32[4,128]{1,0:T(4,128)} %bitcast.3, bf16[32,1024]{1,0:T(8,128)(2,1)} %queries_hbm.1, bf16[3,32,1024]{2,1,0:T(8,128)(2,1)} %memory_hbm.1, s32[3,32]{1,0:T(4,128)} %ages_hbm.1, ...), custom_call_target="tpu_custom_call" | custom-call | tf_op jit(solution)/shard_map/step/pallas_call | solution.py:384
  60.9 0.5 slice_bitcast_fusion
  61.5 1.0 %copy.10 = f32[1024,256]{1,0:T(8,128)} copy(f32[1024,256]{1,0:T(8,128)S(1)} %get-tuple-element.9) | data formatting | bytes 2097152

commit v3 on v2

--- a/solution.py
+++ b/solution.py
@@ -11,8 +11,12 @@
 NX, NY, NC, NZ = 4, 8, 2, 12
 NQ = NY * NC
 DEAD = -1e30
+FAR_Z = (6, 5, 7, 4, 8, 3, 9, 2, 10, 1, 11)
+FAR_Q = (4, 12, 3, 5, 11, 13, 2, 6, 10, 14, 1, 7, 9, 15, 8)
+FAR_X = (2, 1, 3)
 NT = (((1,), (1,)), ((), ()))
 NN = (((1,), (0,)), ((), ()))
+TN = (((0,), (0,)), ((), ()))
 f32, bf16, i32 = jnp.float32, jnp.bfloat16, jnp.int32
 
 
@@ -49,7 +53,7 @@
     loss, grad,
     table, weight, ids, label, ages, meta, marks, cols,
     meta_z, meta_x, mem_x, yq, zq, psend, precv, relayed, pool_x, part, parts, coef_all,
-    count, q4, items, pg_hi, pg_lo,
+    count, q4, items, parted,
     ds, ms, mr, xs, xr, es, er, hs, hr, ys, yr, cs, cr, zs, zr, ps, pr, rs, rr, os, orr, ls, lr, gs, gr,
 ):
     wide = lax.axis_index("wide")
@@ -110,9 +114,12 @@
     def greet(to):
         pl.semaphore_signal(barrier, inc=1, device_id=to, device_id_type=MESH)
 
-    loop(1, NZ, lambda k: greet(zdev(k)))
-    loop(1, NQ, lambda k: greet(qdev(k)))
-    loop(1, NX, lambda k: greet(xdev(k)))
+    for k in FAR_Z:
+        greet(zdev(k))
+    for k in FAR_Q:
+        greet(qdev(k))
+    for k in FAR_X:
+        greet(xdev(k))
 
     ids[4:8] = jnp.zeros((4, 128), i32)
     marks[...] = jnp.zeros((8, 128), i32)
@@ -166,11 +173,13 @@
     def far(j):
         return 6 + (1 - 2 * (j % 2)) * ((j + 1) // 2)
 
-    def near(j):
-        d = 3 - j // 2
-        return jnp.where(j % 2 == 0, d, NZ - d)
-
-    c_meta_z = Copies(lambda k: rc(meta, meta_z.at[z], ms.at[k], mr.at[k], zdev(k)), range(1, NZ))
+    def apart(g, r):
+        u = (r + 1 - z + NZ) % 4
+        if g == 0:
+            return jnp.where(u == 0, NZ - 1, u - 1)
+        return jnp.where(u < 2, u + 3, u + 7) if g == 1 else jnp.where(u < 2, u + 7, u + 3)
+
+    c_meta_z = Copies(lambda k: rc(meta, meta_z.at[z], ms.at[k], mr.at[k], zdev(k)), FAR_Z)
     c_meta_x = Copies(lambda k: rc(meta, meta_x.at[x], xs.at[k], xr.at[k], xdev(k)), range(1, NX))
     c_mem_x = Copies(lambda k: rc(mem_x.at[x], mem_x.at[x], es.at[k], er.at[k], xdev(k)), (1, 3))
     c_half = Copies(half, (0, 1))
@@ -187,14 +196,14 @@
         lambda k: rc(psend.at[k], precv.at[k], ps.at[k], pr.at[k], zdev(k)), (1, 11, 2, 10, 3, 9, 4, 8)
     )
     c_pool = Copies(
-        lambda k: rc(pool_x.at[x], pool_x.at[x], os.at[k], orr.at[k], xdev(k)), (2, 1, 3)
+        lambda k: rc(pool_x.at[x], pool_x.at[x], os.at[k], orr.at[k], xdev(k)), FAR_X
     )
     c_lse = Copies(
         lambda k: rc(part.at[((q + k) % NQ) // 4], parts.at[q], ls.at[k], lr.at[k], qdev(k)),
-        range(1, NQ),
+        FAR_Q,
     )
     c_coef = Copies(
-        lambda k: rc(coef_all.at[z], coef_all.at[z], gs.at[k], gr.at[k], zdev(k)), range(1, NZ)
+        lambda k: rc(coef_all.at[z], coef_all.at[z], gs.at[k], gr.at[k], zdev(k)), FAR_Z
     )
 
     def ring_start(s):
@@ -202,60 +211,68 @@
             recv(c_ring[s - 1])
         start(c_ring[s])
 
-    start(c_meta_z, c_meta_x, c_mem_x, c_q_y, c_across.only(0))
-
-    def partial_sums(owner):
-        wanted = jnp.transpose(meta_z[owner] - base)
-        spots = lax.broadcasted_iota(i32, (nb, rows), 1)
-        found = jnp.zeros((nb, rows), f32)
+    start(c_meta_z, c_q_y.only(5, 3))
+
+    lane = lax.broadcasted_iota(i32, (8, 128), 1) // nb
+
+    def counts(g):
+        lined = [jnp.zeros((8, 128), i32) for b in range(4)]
         for r in range(4):
+            asked = meta_z[wrap(z + apart(g, r), NZ)] - base
             for b in range(4):
-                col = wanted[b * nb : (b + 1) * nb, r : r + 1]
-                found = found + jnp.where(col == spots, 1.0, 0.0)
-        return lax.dot_general(found.astype(bf16), table[...], NN, preferred_element_type=f32)
-
-    recv(c_meta_z.only(3, 9, 2, 10, 1, 11))
-    ring_start(0)
+                rolled = asked if r == b else pltpu.roll(asked, ((r - b) * nb) % 128, 1)
+                lined[b] = jnp.where(lane == r, rolled, lined[b])
+        step = 128
+
+        def block(t):
+            spots = lax.broadcasted_iota(i32, (step, 128), 0) + t * step
+            found = jnp.zeros((step, 128), f32)
+            for b in range(4):
+                for r in range(4):
+                    found = found + jnp.where(lined[b][r : r + 1, :] == spots, 1.0, 0.0)
+            found = found.astype(bf16)
+            spot = pl.ds(pl.multiple_of(t * step, step), step)
+            count[g, spot, 0:128] = found
+            count[g, spot, 128:256] = found
+
+        loop(0, rows // step, block)
+
+    def lookup(g):
+        counts(g)
+        sums = lax.dot_general(count[g, :, 0:128], table[...], TN, preferred_element_type=f32)
+        for r in range(4):
+            psend[apart(g, r)] = sums[r * nb : (r + 1) * nb]
+
+    recv(c_meta_z.only(1, 11, 10))
+    start(c_meta_x, c_mem_x, c_q_y.only(6, 2, 7, 1), c_across.only(0))
     for load in loads[10:]:
         load.wait()
-
-    def lookup_near(j):
-        k = near(j)
-        psend[k] = partial_sums(wrap(z + k, NZ))
-        c_part.make(k).start()
-
-    def lookup_far(j):
-        k = far(j)
-        psend[k] = partial_sums(wrap(z + k, NZ))
-        relay(j).start()
-
-    def lookup_fourth(j):
-        k = far(j)
-        psend[k] = partial_sums(wrap(z + k, NZ))
-
-    loop(0, 6, lookup_near)
-    recv(c_meta_z.only(6, 5, 7, 4, 8))
-    loop(0, 3, lookup_far)
-    recv(c_mem_x)
-    start(c_half)
-    loop(3, 5, lookup_fourth)
-    precv[0] = partial_sums(z)
+    lookup(0)
+    start(c_part.only(1, 11, 2))
+    recv(c_meta_z.only(2, 9, 3, 8))
+    ring_start(0)
+    lookup(1)
+    recv(c_meta_z.only(4, 7, 5, 6))
+    lookup(2)
+    start(c_relay)
+    start(c_part.only(10, 3, 9))
+    recv(c_q_y.only(5))
+    start(c_fourth)
     recv(c_relay)
     psend[4] = psend[4] + (relayed[0] + relayed[1])
     psend[8] = psend[8] + relayed[2]
     start(c_part.only(4, 8))
-    opened.extend([c_part.only(1, 11, 2, 10, 3, 9), c_relay])
     ring_start(1)
 
-    recv(c_q_y.only(5))
-    start(c_fourth)
+    recv(c_mem_x)
+    start(c_half)
     for k in (7, 1, 6, 2, 5, 3):
         if k != 5:
             recv(c_q_y.only(k))
         start(c_across.only(k))
 
     recv(c_part)
-    pooled = precv[0]
+    pooled = psend[0]
     for k in (1, 11, 2, 10, 3, 9, 4, 8):
         pooled = pooled + precv[k]
     pool_x[x] = (pooled / 16.0).astype(bf16)
@@ -305,31 +322,6 @@
     hit = jnp.sum(jnp.where(chosen, own, 0.0), axis=0, keepdims=True)
     lanes = lax.broadcasted_iota(i32, (nb, 128), 1) // nb
 
-    lane = lax.broadcasted_iota(i32, (8, 128), 1) // nb
-
-    def counts(g):
-        ids = []
-        for b in range(4):
-            lined = jnp.zeros((8, 128), i32)
-            for d in range(4):
-                rolled = meta_z[4 * g + d] - base
-                if d != b:
-                    rolled = pltpu.roll(rolled, ((d - b) * nb) % 128, 1)
-                lined = jnp.where(lane == d, rolled, lined)
-            ids.append(lined)
-        step = 128
-
-        def block(t):
-            spots = lax.broadcasted_iota(i32, (step, 128), 0) + t * step
-            found = jnp.zeros((step, 128), f32)
-            for b in range(4):
-                for r in range(4):
-                    found = found + jnp.where(ids[b][r : r + 1, :] == spots, 1.0, 0.0)
-            count[g, pl.ds(pl.multiple_of(t * step, step), step), :] = found.astype(bf16)
-
-        loop(0, rows // step, block)
-
-    counts(0)
     ring_start(4)
     recv(c_lse)
     got = parts[...]
@@ -344,35 +336,38 @@
     coef_all[z] = jnp.where(lanes == z % 4, coef, 0.0).astype(bf16)
     start(c_coef)
     ring_start(5)
-    counts(1)
-    counts(2)
-
-    recv(c_ring[NZ // 2 - 1], c_coef)
-    for g in range(3):
-        held = coef_all[4 * g : 4 * g + 4].reshape(4 * nb, 128)
-        asked = zq[4 * g : 4 * g + 4].reshape(4 * nb, dim)
+
+    def gradient(g):
+        who = [wrap(z + apart(g, r), NZ) for r in range(4)]
+        held = jnp.concatenate([coef_all[w] for w in who], axis=0)
+        asked = jnp.concatenate([zq[w] for w in who], axis=0)
         item_grad = (
             lax.dot_general(held, asked, NN, preferred_element_type=f32) * factor
         ).astype(bf16)
         pooled_grad = lax.dot_general(item_grad, weight[...], NT, preferred_element_type=f32) / 16.0
         upper = pooled_grad.astype(bf16)
-        pg_hi[g] = upper
-        pg_lo[g] = (pooled_grad - upper.astype(f32)).astype(bf16)
-
-    def spread(t):
-        step = 256
-        spot = pl.ds(pl.multiple_of(t * step, step), step)
-        out = jnp.zeros((step, emb), f32)
-        for g in range(3):
-            found = count[g, spot, :]
-            out = out + lax.dot_general(found, pg_hi[g], NN, preferred_element_type=f32)
-            out = out + lax.dot_general(found, pg_lo[g], NN, preferred_element_type=f32)
-        grad[spot, :] = out
-
-    loop(0, rows // 256, spread)
+        parted[0:128, :] = upper
+        parted[128:256, :] = (pooled_grad - upper.astype(f32)).astype(bf16)
+
+        def spread(t):
+            step = 256
+            spot = pl.ds(pl.multiple_of(t * step, step), step)
+            added = lax.dot_general(count[g, spot, :], parted[...], NN, preferred_element_type=f32)
+            grad[spot, :] = added if g == 0 else grad[spot, :] + added
+
+        loop(0, rows // 256, spread)
 
     for kind in opened:
-        kind.sent()
+        if kind is not c_coef and kind is not c_ring[NZ // 2 - 1]:
+            kind.sent()
+    recv(c_coef.only(1, 11, 10))
+    gradient(0)
+    recv(c_coef.only(2, 9, 3, 8))
+    gradient(1)
+    c_coef.sent()
+    c_ring[NZ // 2 - 1].sent()
+    recv(c_ring[NZ // 2 - 1], c_coef.only(4, 7, 5, 6))
+    gradient(2)
 
 
 def body(table, item_weight, ids, queries, memory, slot_age, positive):
@@ -410,11 +405,10 @@
             pltpu.VMEM((4, 8, 128), f32),
             pltpu.VMEM((NQ, 8, 128), f32),
             pltpu.VMEM((NZ, nb, 128), bf16),
-            pltpu.VMEM((3, rows, 128), bf16),
+            pltpu.VMEM((3, rows, 256), bf16),
             pltpu.VMEM((4, nb, dim), bf16),
             pltpu.VMEM((NX * nb, dim), bf16),
-            pltpu.VMEM((3, 128, emb), bf16),
-            pltpu.VMEM((3, 128, emb), bf16),
+            pltpu.VMEM((256, emb), bf16),
             dma((12,)),
             dma((NZ,)), dma((NZ,)),
             dma((NX,)), dma((NX,)),

time: 62.6 us -> 60.5 us (0.966)
  Pallas kernels: 60.3 us -> 57.8 us
    pallas_call x1, Pallas kernels: 60.3 us -> 57.8 us  [body(): pl.pallas_call(kernel, out_shape=(jax.ShapeDtypeStruct((1, 128), f32), ja...]
where the time goes in v3:
time: 60.5 us; the launch traced here: 59.9 us
  Pallas kernels  57.8 us (96%)
  local copies, waits for them, and re-layouts  1.48 us (2%)
  between operations  0.64 us (1%)
    pallas_call x1, Pallas kernels, body(): pl.pallas_call(kernel, out_shape=(jax.ShapeDtypeStruct((1, 128), f32), ja...  57.8 us

profile of v3, /device:TPU:1, one launch (start us, length us, event | category | flops | bytes accessed | tf_op | source)
XLA Modules:
  0.0 59.9 jit_solution(5704657375199962006)
XLA Ops:
  0.6 57.8 %step.1 = (f32[1,128]{1,0:T(1,128)S(1)}, f32[1024,256]{1,0:T(8,128)S(1)}) custom-call(bf16[1024,256]{1,0:T(8,128)(2,1)} %table_hbm.1, bf16[256,1024]{1,0:T(8,128)(2,1)} %weight_hbm.1, s32[4,128]{1,0:T(4,128)} %bitcast.3, bf16[32,1024]{1,0:T(8,128)(2,1)} %queries_hbm.1, bf16[3,32,1024]{2,1,0:T(8,128)(2,1)} %memory_hbm.1, s32[3,32]{1,0:T(4,128)} %ages_hbm.1, ...), custom_call_target="tpu_custom_call" | custom-call | tf_op jit(solution)/shard_map/step/pallas_call | solution.py:379
  58.4 0.5 slice_bitcast_fusion
  58.9 1.0 %copy.10 = f32[1024,256]{1,0:T(8,128)} copy(f32[1024,256]{1,0:T(8,128)S(1)} %get-tuple-element.9) | data formatting | bytes 2097152

commit v4 on v3

--- a/solution.py
+++ b/solution.py
@@ -258,10 +258,12 @@
     start(c_part.only(10, 3, 9))
     recv(c_q_y.only(5))
     start(c_fourth)
-    recv(c_relay)
+    recv(c_relay.only(2))
+    psend[8] = psend[8] + relayed[2]
+    start(c_part.only(8))
+    recv(c_relay.only(1, 0))
     psend[4] = psend[4] + (relayed[0] + relayed[1])
-    psend[8] = psend[8] + relayed[2]
-    start(c_part.only(4, 8))
+    start(c_part.only(4))
     ring_start(1)
 
     recv(c_mem_x)
@@ -331,7 +333,7 @@
     lse = jnp.where(lanes[0:1] == q % 4, lse, 0.0)
     lse = lse + pltpu.roll(lse, 64, 1)
     lse = lse + pltpu.roll(lse, 32, 1)
-    loss[...] = lse - hit
+    loss[...] = (lse - hit)[0, 0:nb]
     coef = jnp.exp(own - lse) - jnp.where(chosen, 1.0, 0.0)
     coef_all[z] = jnp.where(lanes == z % 4, coef, 0.0).astype(bf16)
     start(c_coef)
@@ -379,7 +381,7 @@
     loss, grad = pl.pallas_call(
         kernel,
         out_shape=(
-            jax.ShapeDtypeStruct((1, 128), f32),
+            jax.ShapeDtypeStruct((nb,), f32),
             jax.ShapeDtypeStruct((rows, emb), f32),
         ),
         in_specs=[pl.BlockSpec(memory_space=pltpu.HBM)] * 7,
@@ -428,7 +430,7 @@
         ),
         name="step",
     )(*(pltpu.with_memory_space_constraint(a, pltpu.HBM) for a in arguments))
-    return loss[0, :nb], grad
+    return loss, grad
 
 
 def solution(mesh):

time: 60.5 us -> 60.7 us (level)
    pallas_call x1, Pallas kernels: 57.8 us -> 58.4 us  [body(): pl.pallas_call(kernel, out_shape=(jax.ShapeDtypeStruct((nb,), f32), jax.S...]
    unnamed x1 -> x2, local copies, waits for them, and re-layouts: 0.97 us -> 1.48 us
where the time goes in v4:
time: 60.7 us; the launch traced here: 60.5 us
  Pallas kernels  58.4 us (96%)
  local copies, waits for them, and re-layouts  1.48 us (2%)
  between operations  0.64 us (1%)
    pallas_call x1, Pallas kernels, body(): pl.pallas_call(kernel, out_shape=(jax.ShapeDtypeStruct((nb,), f32), jax.S...  58.4 us
    unnamed x2, local copies, waits for them, and re-layouts  1.48 us

profile of v4, /device:TPU:1, one launch (start us, length us, event | category | flops | bytes accessed | tf_op | source)
XLA Modules:
  0.0 60.5 jit_solution(2316927767319559482)
XLA Ops:
  0.6 58.4 %step.1 = (f32[32]{0:T(128)S(1)}, f32[1024,256]{1,0:T(8,128)S(1)}) custom-call(bf16[1024,256]{1,0:T(8,128)(2,1)} %table_hbm.1, bf16[256,1024]{1,0:T(8,128)(2,1)} %weight_hbm.1, s32[4,128]{1,0:T(4,128)} %bitcast.1, bf16[32,1024]{1,0:T(8,128)(2,1)} %queries_hbm.1, bf16[3,32,1024]{2,1,0:T(8,128)(2,1)} %memory_hbm.1, s32[3,32]{1,0:T(4,128)} %ages_hbm.1, ...), custom_call_target="tpu_custom_call" | custom-call | tf_op jit(solution)/shard_map/step/pallas_call | solution.py:381
  59.0 0.5 copy.11
  59.5 1.0 %copy.12 = f32[1024,256]{1,0:T(8,128)} copy(f32[1024,256]{1,0:T(8,128)S(1)} %get-tuple-element.5) | data formatting | bytes 2097152

commit v5 on v4

--- a/solution.py
+++ b/solution.py
@@ -352,12 +352,12 @@
         parted[128:256, :] = (pooled_grad - upper.astype(f32)).astype(bf16)
 
         def spread(t):
-            step = 256
+            step = 512
             spot = pl.ds(pl.multiple_of(t * step, step), step)
             added = lax.dot_general(count[g, spot, :], parted[...], NN, preferred_element_type=f32)
             grad[spot, :] = added if g == 0 else grad[spot, :] + added
 
-        loop(0, rows // 256, spread)
+        loop(0, rows // 512, spread)
 
     for kind in opened:
         if kind is not c_coef and kind is not c_ring[NZ // 2 - 1]:

time: 60.7 us -> 59.9 us (0.987)
  Pallas kernels: 58.4 us -> 57.5 us
    pallas_call x1, Pallas kernels: 58.4 us -> 57.5 us  [body(): pl.pallas_call(kernel, out_shape=(jax.ShapeDtypeStruct((nb,), f32), jax.S...]
where the time goes in v5:
time: 59.9 us; the launch traced here: 59.6 us
  Pallas kernels  57.5 us (96%)
  local copies, waits for them, and re-layouts  1.48 us (2%)
  between operations  0.64 us (1%)
    pallas_call x1, Pallas kernels, body(): pl.pallas_call(kernel, out_shape=(jax.ShapeDtypeStruct((nb,), f32), jax.S...  57.5 us
    unnamed x2, local copies, waits for them, and re-layouts  1.48 us

profile of v5, /device:TPU:1, one launch (start us, length us, event | category | flops | bytes accessed | tf_op | source)
XLA Modules:
  0.0 59.6 jit_solution(15714858687678509376)
XLA Ops:
  0.6 57.5 %step.1 = (f32[32]{0:T(128)S(1)}, f32[1024,256]{1,0:T(8,128)S(1)}) custom-call(bf16[1024,256]{1,0:T(8,128)(2,1)} %table_hbm.1, bf16[256,1024]{1,0:T(8,128)(2,1)} %weight_hbm.1, s32[4,128]{1,0:T(4,128)} %bitcast.1, bf16[32,1024]{1,0:T(8,128)(2,1)} %queries_hbm.1, bf16[3,32,1024]{2,1,0:T(8,128)(2,1)} %memory_hbm.1, s32[3,32]{1,0:T(4,128)} %ages_hbm.1, ...), custom_call_target="tpu_custom_call" | custom-call | tf_op jit(solution)/shard_map/step/pallas_call | solution.py:381
  58.1 0.5 copy.11
  58.6 1.0 %copy.12 = f32[1024,256]{1,0:T(8,128)} copy(f32[1024,256]{1,0:T(8,128)S(1)} %get-tuple-element.5) | data formatting | bytes 2097152
